TPU v7x, 512 devices: a whole 4x4x16 slice. The times are simulated.
512 devices in a mesh: lab: 32 (over z_lo, y, core), img: 16 (over x, z_hi).
Axes of the slice: x: 4, y: 4, z: 16 (z_hi: 4, z_lo: 4; z = z_hi * 4 + z_lo), core: 2. Of those that a mesh axis runs over, the one named last changes fastest.
Arguments:
- queries: bfloat16 [32768, 512], P('lab'), may hold values from -12 to 12
- keys: bfloat16 [16, 576, 512], P('img', 'lab'), may hold values from -5 to 5
- values: bfloat16 [16, 576, 512], P('img', 'lab'), may hold values from -6 to 6
- grad_out: bfloat16 [16, 32768, 512], P('img', 'lab'), may hold values from -6 to 6
- block_mask: int32 [256, 16], P('lab', 'img'), may hold values from 0 to 1, as said below
Outputs:
- grad_queries: bfloat16 [32768, 512], P(('lab', 'img'))
- grad_keys: bfloat16 [16, 576, 512], P('img', 'lab')
- grad_values: bfloat16 [16, 576, 512], P('img', 'lab')
Inputs may be any that keep to these rules, and one draw needn't show every extreme that they name: `block_mask`: each label block has its own density of images that it reads.
All inputs are finite; a program needn't handle non-finite values.
Results may differ from a plain program's by a relative error of at most 0.0061.
Values may be sent and summed in bfloat16 or wider, within the bound.
A program may use at most 128 MiB of HBM per device.

v0:
```python
import math

import jax
import jax.numpy as jnp
from jax import lax
from jax.sharding import PartitionSpec as P

H = 8
E = 64


def attend(query_block, grad_block, key_image, value_image, weight):
    scale = 1.0 / math.sqrt(E)
    scores = (
        jnp.einsum("lhe,phe->lhp", query_block, key_image, preferred_element_type=jnp.float32)
        * scale
    )
    probs = jax.nn.softmax(scores, axis=-1)
    dprobs = jnp.einsum("lhe,phe->lhp", grad_block, value_image, preferred_element_type=jnp.float32)
    delta = jnp.sum(probs * dprobs, axis=-1, keepdims=True)
    masked = (probs * weight).astype(jnp.bfloat16)
    dscores = (weight * probs * (dprobs - delta) * scale).astype(jnp.bfloat16)
    query_grad = jnp.einsum("lhp,phe->lhe", dscores, key_image, preferred_element_type=jnp.float32)
    return (masked, dscores, query_grad)


def body(queries, keys, values, grad_out, block_mask):
    lab_rows, feature_width = queries.shape
    blocks = block_mask.shape[0]
    img_count = keys.shape[0]
    block_rows = lab_rows // blocks
    keys_full, values_full = (
        lax.all_gather(keys, "lab", axis=1, tiled=True),
        lax.all_gather(values, "lab", axis=1, tiled=True),
    )
    patches = keys_full.shape[1]
    query_blocks = queries.reshape(blocks, block_rows, H, E)
    grad_blocks = grad_out.reshape(img_count, blocks, block_rows, H, E)
    weights = block_mask.astype(jnp.float32)
    key_image = keys_full[0].reshape(patches, H, E)
    value_image = values_full[0].reshape(patches, H, E)

    def run_block(carry, pieces):
        query_block, grad_block, weight = pieces
        masked, dscores, query_grad = attend(
            query_block, grad_block, key_image, value_image, weight
        )
        dk_acc, dv_acc = carry
        dk_acc = dk_acc + jnp.einsum(
            "lhp,lhe->phe", dscores, query_block, preferred_element_type=jnp.float32
        )
        dv_acc = dv_acc + jnp.einsum(
            "lhp,lhe->phe", masked, grad_block, preferred_element_type=jnp.float32
        )
        return ((dk_acc, dv_acc), query_grad)

    zero_acc = jnp.zeros((patches, H, E), jnp.float32)
    (dk_acc, dv_acc), query_grads = lax.scan(
        run_block, (zero_acc, zero_acc), (query_blocks, grad_blocks[0], weights[:, 0])
    )
    key_terms = [dk_acc.reshape(patches, feature_width)]
    value_terms = [dv_acc.reshape(patches, feature_width)]
    key_stack = jnp.stack(key_terms)
    value_stack = jnp.stack(value_terms)
    key_sum = lax.psum_scatter(key_stack, "lab", scatter_dimension=1, tiled=True)
    value_sum = lax.psum_scatter(value_stack, "lab", scatter_dimension=1, tiled=True)
    grad_keys = key_sum.astype(jnp.bfloat16)
    grad_values = value_sum.astype(jnp.bfloat16)
    summed = lax.psum_scatter(
        query_grads.reshape(lab_rows, feature_width), "img", scatter_dimension=0, tiled=True
    )
    grad_queries = summed.astype(jnp.bfloat16)
    return (grad_queries, grad_keys, grad_values)


def solution(mesh):
    return jax.shard_map(
        body,
        mesh=mesh,
        in_specs=(
            P("lab", None),
            P("img", "lab", None),
            P("img", "lab", None),
            P("img", "lab", None),
            P("lab", "img"),
        ),
        out_specs=(P(("lab", "img"), None), P("img", "lab", None), P("img", "lab", None)),
        check_vma=False,
    )
```

profile of v0, /device:TPU:6, one launch (start us, length us, event | category | flops | bytes accessed | tf_op | source)
XLA Modules:
  0.0 573.6 jit_solution(8856966647616170280)
XLA Ops:
  15.1 47.8 %all_gather.6 = bf16[1,576,512]{2,0,1:T(2,128)(2,1)S(1)} all-gather(bf16[1,18,512]{2,0,1:T(2,128)(2,1)S(1)} %copy.38), channel_id=1, replica_groups=mesh['lab'=32,'img'=16] {'lab'}, dimensions={1}, use_global_device_ids=true | all-gather | bytes 608256 | tf_op jit(solution)/shard_map/all_gather | solution.py:33
  65.4 41.1 %all_gather.7 = bf16[1,576,512]{2,0,1:T(2,128)(2,1)S(1)} all-gather(bf16[1,18,512]{2,0,1:T(2,128)(2,1)S(1)} %copy.41), channel_id=1, replica_groups=mesh['lab'=32,'img'=16] {'lab'}, dimensions={1}, use_global_device_ids=true | all-gather | bytes 608256 | tf_op jit(solution)/shard_map/all_gather | solution.py:34
  108.1 162.1 %while.15 = (s32[]{:T(128)}, f32[576,8,64]{0,2,1:T(8,128)}, f32[576,8,64]{0,2,1:T(8,128)}, f32[8,128,8,64]{1,3,2,0:T(8,128)}, bf16[8,128,8,64]{1,3,2,0:T(8,128)(...) while((s32[]{:T(128)}, f32[576,8,64]{0,2,1:T(8,128)}, ...), condition=%wide.region_4.5_spmd.clone, body=%wide.region_0.4_spmd.clone.sunk | while | flops 391646912 | bytes 33648772 | solution.py:58
  108.1 3.6 fusion.79
  113.8 4.9 fusion.82
  118.6 4.0 fusion.81
  122.7 5.1 fusion.80
  133.4 4.9 fusion.82
  138.3 4.4 fusion.81
  142.7 5.5 fusion.80
  153.8 4.9 fusion.82
  158.6 4.4 fusion.81
  163.0 5.5 fusion.80
  174.1 4.9 fusion.82
  179.0 4.4 fusion.81
  183.4 5.5 fusion.80
  194.5 4.9 fusion.82
  199.3 4.4 fusion.81
  203.7 5.5 fusion.80
  214.8 4.9 fusion.82
  219.7 4.4 fusion.81
  224.1 5.5 fusion.80
  235.2 4.8 fusion.82
  240.0 4.4 fusion.81
  244.4 5.5 fusion.80
  255.5 4.9 fusion.82
  260.4 4.4 fusion.81
  264.7 5.5 fusion.80
  270.2 3.9 copy.57
  274.1 4.8 reshape.19
  286.3 251.8 %all-reduce.4 = (bf16[1,576,512]{2,0,1:T(2,128)(2,1)S(1)}, bf16[1,576,512]{2,0,1:T(2,128)(2,1)}) all-reduce(f32[1,576,512]{2,0,1:T(1,128)S(1)} %copy.46, f32[1,576,512]{2,0,1:T(1,128)S(1)} %copy.47), channel_id=3, replica_groups=mesh['lab'=32,'img'=16] {'lab'}, use_global_device_ids=true, to_apply=%region_6.7.clone | all-reduce | flops 589824 | bytes 3538944
  540.1 24.9 %reduce-scatter.4.cloned.1.call-done = f32[64,512]{1,0:T(8,128)} async-done(((f32[1024,512]{1,0:T(8,128)}), f32[64,512]{1,0:T(8,128)}) %reduce-scatter.4.cloned.1.call-update) | async-done | bytes 131088
  (55 shorter events, 64.0 us)
Async XLA Ops:
  7.2 557.9 %reduce-scatter.4.cloned.1.call-start = ((), (), s32[]{:S(2)}) async-start(), calls=%async_computation.1 | async-start | bytes 2228224
  7.2 4.8 copy-start.1
  12.1 3.0 copy-start.2
  13.2 52.2 %copy-start.3 = (bf16[1,18,512]{2,1,0:T(8,128)(2,1)S(1)}, bf16[1,18,512]{2,1,0:T(8,128)(2,1)}, u32[]{:S(2)}) copy-start(bf16[1,18,512]{2,1,0:T(8,128)(2,1)} %param.9) | copy-start | bytes 55300
  62.9 45.2 %copy-start.4 = (s32[8,1]{0,1:T(1,128)S(1)}, s32[8,1]{0,1:T(1,128)}, u32[]{:S(2)}) copy-start(s32[8,1]{0,1:T(1,128)} %param.11) | copy-start | bytes 100
  278.8 1.3 copy-start
Sparse Core Ops, SparseCore 0:
  279.0 285.9 reduce-scatter.3
where the time goes:
time: 576 us; the launch traced here: 574 us
  blocking collectives  341 us (59%)
  matrix products  157 us (27%)
  local copies, waits for them, and re-layouts  35.8 us (6%)
  waiting for transfers between devices  24.9 us (4%)
  between operations  14.8 us (3%)
    unnamed x1, blocking collectives  252 us
    all_gather x1, blocking collectives, body(): lax.all_gather(keys, 'lab', axis=1, tiled=True)  47.8 us
    dot_general x8, matrix products, run_block(): jnp.einsum('lhp,lhe->phe', dscores, query_block, preferred_element_type=j...  43.4 us
    all_gather x1, blocking collectives, body(): lax.all_gather(values, 'lab', axis=1, tiled=True)  41.1 us
    dot_general x8, matrix products, attend(): jnp.einsum('lhp,phe->lhe', dscores, key_image, preferred_element_type=jnp...  38.9 us
    dot_general x8, matrix products, run_block(): jnp.einsum('lhp,lhe->phe', masked, grad_block, preferred_element_type=jnp...  34.7 us
    sub x8, matrix products, attend(): probs = jax.nn.softmax(scores, axis=-1)  28.7 us
    unnamed x2, waiting for transfers between devices  24.9 us
  transfers between devices with their start and end apart: 1, of which 1 were waited for; matrix products, arithmetic and copies ran while one was open for 1% of the time, Pallas kernels for 0%

commit v1 on v0

v1 whole, which is shorter than its diff:
```python
import functools
import math

import jax
import jax.numpy as jnp
from jax import lax
from jax.experimental import pallas as pl
from jax.experimental.pallas import tpu as pltpu
from jax.sharding import PartitionSpec as P

F32, BF16 = jnp.float32, jnp.bfloat16
MESH = pl.DeviceIdType.MESH
SCALE = 0.125
EXP2_SCALE = SCALE * math.log2(math.e)
PAIRS = 4
CH = 256
SIZES = (4, 4, 4, 4)


def dot(a, b, ca, cb):
    return lax.dot_general(a, b, (((ca,), (cb,)), ((), ())), preferred_element_type=F32)


def kernel(
    sizes,
    mask_ref,
    key_ref,
    val_ref,
    q_hbm,
    g_hbm,
    dq_out,
    dk_out,
    dv_out,
    q_v,
    g_v,
    kv,
    tl,
    tl_f,
    kt,
    acc,
    s_buf,
    d_buf,
    e_buf,
    mx_buf,
    dq_own,
    sx,
    rx,
    sz,
    rz,
    z_own,
    sa,
    ra,
    sb,
    rb,
    tb,
    sc,
    rc,
    st,
    rt,
    ft,
    in_sem,
    ag_send,
    ag_recv,
    agt_send,
    agt_recv,
    x_send,
    x_recv,
    h_send,
    h_recv,
    a_send,
    a_recv,
    b_send,
    b_recv,
    c_send,
    c_recv,
    t_send,
    t_recv,
):
    NZ, NY, NX, NH = sizes
    NS = NZ * NY
    NLAB = 2 * NS
    MAIN = 16 * NLAB
    ROWS = 18 * NLAB
    STEPS = PAIRS * NX
    HB = CH // NH
    ZR = NZ * 16
    HALF = NS * 16
    TH = NS * 2
    TZ = NZ * 2

    a = lax.axis_index("lab")
    i = lax.axis_index("img")
    z = a // (2 * NY)
    y = (a // 2) % NY
    c = a % 2
    x = i // NH
    zh = i % NH
    slot = c * NS + y * NZ + z

    def lab_id(z_, y_, c_):
        return {"lab": z_ * (2 * NY) + y_ * 2 + c_}

    def img_id(x_, h_):
        return {"img": x_ * NH + h_}

    def dev_z(d):
        return lab_id((z + d) % NZ, y, c)

    def dev_y(d):
        return lab_id(z, (y + d) % NY, c)

    def dev_c():
        return lab_id(z, y, 1 - c)

    def dev_x(d):
        return img_id((x + d) % NX, zh)

    def dev_h(d):
        return img_id(x, (zh + d) % NH)

    def rcopy(src, dst, ssem, rsem, dev):
        return pltpu.make_async_remote_copy(
            src_ref=src, dst_ref=dst, send_sem=ssem, recv_sem=rsem, device_id=dev, device_id_type=MESH
        )

    peers = [dev_c()]
    peers += [dev_z(d) for d in range(1, NZ)]
    peers += [dev_y(d) for d in range(1, NY)]
    peers += [dev_x(d) for d in range(1, NX)]
    peers += [dev_h(d) for d in range(1, NH)]
    barrier = pltpu.get_barrier_semaphore()
    for dev in peers:
        pl.semaphore_signal(barrier, inc=1, device_id=dev, device_id_type=MESH)

    def in_copies(j):
        lanes = pl.ds(pl.multiple_of(j * 128, 128), 128)
        return (
            pltpu.make_async_copy(q_hbm.at[:, lanes], q_v.at[j], in_sem.at[0, j]),
            pltpu.make_async_copy(g_hbm.at[0, :, lanes], g_v.at[j], in_sem.at[1, j]),
        )

    for j in range(PAIRS):
        for cp in in_copies(j):
            cp.start()

    for n, ref in ((0, key_ref), (1, val_ref)):
        for j in range(PAIRS):
            lanes = slice(j * 128, (j + 1) * 128)
            kv[j, n, pl.ds(pl.multiple_of(slot * 16, 16), 16), :] = ref[0, 0:16, lanes]
            tl_f[pl.ds(n * 8 + j * 2, 2), :] = ref[0, 16:18, lanes].astype(F32)
    tl[pl.ds(pl.multiple_of(slot * 16, 16), 16), :] = tl_f[...].astype(BF16)
    pl.semaphore_wait(barrier, len(peers))

    def ag_z(j, d):
        r = kv.at[j, :, pl.ds(pl.multiple_of(slot * 16, 16), 16), :]
        return rcopy(r, r, ag_send.at[j, d - 1], ag_recv.at[j, d - 1], dev_z(d))

    def ag_y(j, d):
        r = kv.at[j, :, pl.ds(pl.multiple_of(c * HALF + y * ZR, 16), ZR), :]
        n = NZ - 1 + d - 1
        return rcopy(r, r, ag_send.at[j, n], ag_recv.at[j, n], dev_y(d))

    def ag_c(j):
        r = kv.at[j, :, pl.ds(pl.multiple_of(c * HALF, 16), HALF), :]
        n = NZ + NY - 2
        return rcopy(r, r, ag_send.at[j, n], ag_recv.at[j, n], dev_c())

    def agt_z(d):
        r = tl.at[pl.ds(pl.multiple_of(slot * 16, 16), 16), :]
        return rcopy(r, r, agt_send.at[d - 1], agt_recv.at[d - 1], dev_z(d))

    def agt_y(d):
        r = tl.at[pl.ds(pl.multiple_of(c * HALF + y * ZR, 16), ZR), :]
        n = NZ - 1 + d - 1
        return rcopy(r, r, agt_send.at[n], agt_recv.at[n], dev_y(d))

    def agt_c():
        r = tl.at[pl.ds(pl.multiple_of(c * HALF, 16), HALF), :]
        n = NZ + NY - 2
        return rcopy(r, r, agt_send.at[n], agt_recv.at[n], dev_c())

    def z_to_y(j):
        for d in range(1, NZ):
            ag_z(j, d).wait_recv()
        for d in range(1, NY):
            ag_y(j, d).start()

    def y_to_c(j):
        for d in range(1, NY):
            ag_y(j, d).wait_recv()
        ag_c(j).start()

    for d in range(1, NZ):
        agt_z(d).start()
        ag_z(0, d).start()
    for j in range(1, PAIRS):
        for d in range(1, NZ):
            ag_z(j, d).start()

    for j in range(PAIRS):
        for n in range(2):
            acc[j, n] = jnp.zeros((ROWS, 128), F32)

    for d in range(1, NZ):
        agt_z(d).wait_recv()
    for d in range(1, NY):
        agt_y(d).start()
    z_to_y(0)
    z_to_y(1)
    tails = 16 * NLAB
    row = lax.broadcasted_iota(jnp.int32, (tails, tails), 0)
    col = lax.broadcasted_iota(jnp.int32, (tails, tails), 1)
    per = 2 * NLAB
    want = ((row % per) // 2) * 16 + ((row // per) % 2) * 8 + (row // (2 * per)) * 2 + row % 2
    order = jnp.where(col == want, 1.0, 0.0).astype(BF16)
    for d in range(1, NY):
        agt_y(d).wait_recv()
    agt_c().start()
    y_to_c(0)
    for j in range(2, PAIRS):
        z_to_y(j)
    agt_c().wait_recv()
    placed = dot(order, tl[...], 1, 0).astype(BF16)
    for j in range(PAIRS):
        for n in range(2):
            b0 = (j * 2 + n) * per
            kv[j, n, MAIN:ROWS, :] = placed[b0 : b0 + per, :]

    def turn_keys(j):
        kt[j] = jnp.transpose(kv[j, 0].astype(F32)).astype(BF16)

    def ready(j):
        ag_c(j).wait_recv()
        for cp in in_copies(j):
            cp.wait()
        turn_keys(j)

    ready(0)

    lane = lax.broadcasted_iota(jnp.int32, (1, 128), 1)

    def of_head(h, v):
        sel = (lane < 64) if h == 0 else (lane >= 64)
        return jnp.where(sel, v, jnp.zeros_like(v))

    def operands(s):
        s = s % STEPS
        j = s // NX
        chunk = (x + 1 + s % NX) % NX
        rows = pl.ds(pl.multiple_of(chunk * CH, CH), CH)
        return j, chunk, q_v[j, rows, :], g_v[j, rows, :]

    def front(s, h):
        j, _, q, g = operands(s)
        sv = dot(kv[j, 0], of_head(h, q), 1, 1)
        s_buf[h] = sv
        d_buf[h] = dot(kv[j, 1], of_head(h, g), 1, 1)
        mx_buf[h] = jnp.max(sv, axis=0, keepdims=True)

    def middle(h):
        e = jnp.exp2((s_buf[h] - mx_buf[h]) * EXP2_SCALE)
        e_buf[h] = e
        return jnp.sum(e, axis=0, keepdims=True), jnp.sum(e * d_buf[h], axis=0, keepdims=True)

    def back(h, j, q, g, m, total, weighted):
        qm, gm = of_head(h, q), of_head(h, g)
        t = e_buf[h] * (m / total)
        masked = t.astype(BF16)
        ds = (t * (d_buf[h] - weighted / total)).astype(BF16)
        acc[j, 0] += dot(ds, qm, 1, 0)
        acc[j, 1] += dot(masked, gm, 1, 0)
        return dot(kt[j, h * 64 : (h + 1) * 64, :], ds, 1, 0)

    def rs_a(j):
        return rcopy(sa.at[j], ra.at[j], a_send.at[j], a_recv.at[j], dev_c())

    def rs_b(j, d):
        return rcopy(sb.at[j, d - 1], rb.at[j, d - 1], b_send.at[j, d - 1], b_recv.at[j, d - 1], dev_y(d))

    def rs_c(j, d):
        return rcopy(sc.at[j, d - 1], rc.at[j, d - 1], c_send.at[j, d - 1], c_recv.at[j, d - 1], dev_z(d))

    def rs_t(d):
        return rcopy(st.at[(z + d) % NZ], rt.at[d - 1], t_send.at[d - 1], t_recv.at[d - 1], dev_z(d))

    def stage_a(j):
        other = 1 - c
        for n in range(2):
            sa[j, n, 0:HALF, :] = acc[j, n, pl.ds(pl.multiple_of(other * HALF, 16), HALF), :].astype(BF16)
            sa[j, n, HALF : HALF + TH, :] = acc[
                j, n, pl.ds(pl.multiple_of(MAIN + other * TH, 8), TH), :
            ].astype(BF16)
        rs_a(j).start()

    def stage_b(j):
        rs_a(j).wait_recv()
        for d in list(range(1, NY)) + [0]:
            yy = (y + d) % NY
            tail = []
            for n in range(2):
                at = pl.ds(pl.multiple_of(c * HALF + yy * ZR, 16), ZR)
                got = ra[j, n, pl.ds(pl.multiple_of(yy * ZR, 16), ZR), :].astype(F32)
                both = acc[j, n, at, :] + got
                tat = pl.ds(pl.multiple_of(MAIN + c * TH + yy * TZ, 8), TZ)
                tail.append(acc[j, n, tat, :])
                if d == 0:
                    acc[j, n, at, :] = both
                else:
                    sb[j, d - 1, n * ZR : (n + 1) * ZR, :] = both.astype(BF16)
            tmine = jnp.concatenate(tail, axis=0)
            for n in range(2):
                full = ra[j, n, HALF : HALF + TH, :].astype(F32)
                ft[n] = full
            tgot = jnp.concatenate(
                [ft[n, pl.ds(pl.multiple_of(yy * TZ, 8), TZ), :] for n in range(2)], axis=0
            )
            if d == 0:
                tb[j] = tmine + tgot
            else:
                sb[j, d - 1, 2 * ZR : 2 * ZR + 2 * TZ, :] = (tmine + tgot).astype(BF16)
                rs_b(j, d).start()

    def stage_c(j):
        for d in range(1, NY):
            rs_b(j, d).wait_recv()
        for n in range(2):
            at = pl.ds(pl.multiple_of(c * HALF + y * ZR, 16), ZR)
            v = acc[j, n, at, :]
            for d in range(1, NY):
                v = v + rb[j, d - 1, n * ZR : (n + 1) * ZR, :].astype(F32)
            acc[j, n, at, :] = v
        v = tb[j]
        for d in range(1, NY):
            v = v + rb[j, d - 1, 2 * ZR : 2 * ZR + 2 * TZ, :].astype(F32)
        tb[j] = v
        for d in range(1, NZ):
            zz = (z + d) % NZ
            for n in range(2):
                at = pl.ds(pl.multiple_of(c * HALF + y * ZR + zz * 16, 16), 16)
                sc[j, d - 1, n * 16 : (n + 1) * 16, :] = acc[j, n, at, :].astype(BF16)
            rs_c(j, d).start()

    def final_kv(j):
        for d in range(1, NZ):
            rs_c(j, d).wait_recv()
        lanes = pl.ds(pl.multiple_of(j * 128, 128), 128)
        for n, out in ((0, dk_out), (1, dv_out)):
            v = acc[j, n, pl.ds(pl.multiple_of(slot * 16, 16), 16), :]
            for d in range(1, NZ):
                v = v + rc[j, d - 1, n * 16 : (n + 1) * 16, :].astype(F32)
            if n == 0:
                v = v * SCALE
            out[0, 0:16, lanes] = v.astype(BF16)

    def rs_x(j, t):
        return rcopy(sx.at[j, t], rx.at[j, t], x_send.at[j, t], x_recv.at[j, t], dev_x(t + 1))

    def rs_h(j, d):
        return rcopy(sz.at[j, d - 1], rz.at[j, d - 1], h_send.at[j, d - 1], h_recv.at[j, d - 1], dev_h(d))

    def stage_h(j):
        for t in range(NX - 1):
            rs_x(j, t).wait_recv()
        v = dq_own[j]
        for t in range(NX - 1):
            v = v + rx[j, t].astype(F32)
        z_own[j] = jnp.transpose(v)
        for d in range(1, NH):
            hh = (zh + d) % NH
            sz[j, d - 1] = z_own[j, pl.ds(pl.multiple_of(hh * HB, HB), HB), :].astype(BF16)
            rs_h(j, d).start()

    def final_q(j):
        for d in range(1, NH):
            rs_h(j, d).wait_recv()
        v = z_own[j, pl.ds(pl.multiple_of(zh * HB, HB), HB), :]
        for d in range(1, NH):
            v = v + rz[j, d - 1].astype(F32)
        lanes = pl.ds(pl.multiple_of(j * 128, 128), 128)
        dq_out[:, lanes] = (v * SCALE).astype(BF16)

    front(0, 0)

    def body(s, carry):
        j = s // NX
        t = s % NX

        @pl.when(jnp.logical_and(t == min(1, NX - 2), j < PAIRS - 1))
        def _():
            y_to_c(j + 1)

        @pl.when(jnp.logical_and(t == NX - 1, j < PAIRS - 1))
        def _():
            ready(j + 1)

        _, chunk, q, g = operands(s)
        m = jnp.concatenate(
            [
                jnp.full((1, 128), mask_ref[chunk * (CH // 128) + b, 0], jnp.int32).astype(F32)
                for b in range(CH // 128)
            ],
            axis=1,
        )
        front(s, 1)
        total, weighted = middle(0)
        dq0 = back(0, j, q, g, m, total, weighted)
        front(s + 1, 0)
        total, weighted = middle(1)
        dq1 = back(1, j, q, g, m, total, weighted)

        @pl.when(t < NX - 1)
        def _():
            for u in range(NX - 1):

                @pl.when(t == u)
                def _():
                    sx[j, u, 0:64, :] = dq0.astype(BF16)
                    sx[j, u, 64:128, :] = dq1.astype(BF16)
                    rs_x(j, u).start()

        @pl.when(t == NX - 1)
        def _():
            dq_own[j, 0:64, :] = dq0
            dq_own[j, 64:128, :] = dq1
            stage_a(j)

        @pl.when(jnp.logical_and(t == 0, j > 0))
        def _():
            stage_h(j - 1)
            stage_b(j - 1)

        @pl.when(jnp.logical_and(t == max(NX - 2, 1), j > 0))
        def _():
            stage_c(j - 1)

        @pl.when(jnp.logical_and(t == NX - 1, j > 0))
        def _():
            final_kv(j - 1)
            final_q(j - 1)

        return carry

    lax.fori_loop(0, STEPS, body, 0)

    last = PAIRS - 1
    stage_h(last)
    stage_b(last)
    stage_c(last)
    n_t = PAIRS * 2 * TZ
    row = lax.broadcasted_iota(jnp.int32, (n_t, n_t), 0)
    col = lax.broadcasted_iota(jnp.int32, (n_t, n_t), 1)
    want = ((row // 4) % PAIRS) * (2 * TZ) + ((row // 2) % 2) * TZ + (row // 16) * 2 + row % 2
    order = jnp.where(col == want, 1.0, 0.0).astype(BF16)
    mine = jnp.concatenate([tb[j].astype(BF16) for j in range(PAIRS)], axis=0)
    sorted_tails = dot(order, mine, 1, 0).astype(BF16)
    for zz in range(NZ):
        st[zz] = sorted_tails[zz * 16 : (zz + 1) * 16, :]
    for d in range(1, NZ):
        rs_t(d).start()
    final_kv(last)
    for d in range(1, NZ):
        rs_t(d).wait_recv()
    v = st[z].astype(F32)
    for d in range(1, NZ):
        v = v + rt[d - 1].astype(F32)
    tl_f[...] = v
    for n, out in ((0, dk_out), (1, dv_out)):
        for j in range(PAIRS):
            piece = tl_f[pl.ds(j * 4 + n * 2, 2), :]
            if n == 0:
                piece = piece * SCALE
            out[0, 16:18, j * 128 : (j + 1) * 128] = piece.astype(BF16)
    final_q(last)

    for d in range(1, NZ):
        agt_z(d).wait_send()
        rs_t(d).wait_send()
    for d in range(1, NY):
        agt_y(d).wait_send()
    agt_c().wait_send()

    def drain(j, carry):
        for d in range(1, NZ):
            ag_z(j, d).wait_send()
            rs_c(j, d).wait_send()
        for d in range(1, NY):
            ag_y(j, d).wait_send()
            rs_b(j, d).wait_send()
        ag_c(j).wait_send()
        rs_a(j).wait_send()
        for t in range(NX - 1):
            rs_x(j, t).wait_send()
        for d in range(1, NH):
            rs_h(j, d).wait_send()
        return carry

    lax.fori_loop(0, PAIRS, drain, 0)


def body_of(sizes):
    NZ, NY, NX, NH = sizes
    NS = NZ * NY
    NLAB = 2 * NS
    ROWS = 18 * NLAB
    HB = CH // NH
    LABELS = CH * NX
    ZR, TZ = NZ * 16, NZ * 2
    dma = pltpu.SemaphoreType.DMA

    def body(queries, keys, values, grad_out, block_mask):
        vm = pl.BlockSpec(memory_space=pltpu.VMEM)
        sm = pl.BlockSpec(memory_space=pltpu.SMEM)
        anywhere = pl.BlockSpec(memory_space=pl.ANY)
        scratch = [
            pltpu.VMEM((PAIRS, LABELS, 128), BF16),
            pltpu.VMEM((PAIRS, LABELS, 128), BF16),
            pltpu.VMEM((PAIRS, 2, ROWS, 128), BF16),
            pltpu.VMEM((16 * NLAB, 128), BF16),
            pltpu.VMEM((16, 128), F32),
            pltpu.VMEM((PAIRS, 128, ROWS), BF16),
            pltpu.VMEM((PAIRS, 2, ROWS, 128), F32),
            pltpu.VMEM((2, ROWS, CH), F32),
            pltpu.VMEM((2, ROWS, CH), F32),
            pltpu.VMEM((2, ROWS, CH), F32),
            pltpu.VMEM((2, 1, CH), F32),
            pltpu.VMEM((PAIRS, 128, CH), F32),
            pltpu.VMEM((PAIRS, NX - 1, 128, CH), BF16),
            pltpu.VMEM((PAIRS, NX - 1, 128, CH), BF16),
            pltpu.VMEM((PAIRS, NH - 1, HB, 128), BF16),
            pltpu.VMEM((PAIRS, NH - 1, HB, 128), BF16),
            pltpu.VMEM((PAIRS, CH, 128), F32),
            pltpu.VMEM((PAIRS, 2, NS * 18, 128), BF16),
            pltpu.VMEM((PAIRS, 2, NS * 18, 128), BF16),
            pltpu.VMEM((PAIRS, NY - 1, 2 * ZR + 2 * TZ, 128), BF16),
            pltpu.VMEM((PAIRS, NY - 1, 2 * ZR + 2 * TZ, 128), BF16),
            pltpu.VMEM((PAIRS, 2 * TZ, 128), F32),
            pltpu.VMEM((PAIRS, NZ - 1, 32, 128), BF16),
            pltpu.VMEM((PAIRS, NZ - 1, 32, 128), BF16),
            pltpu.VMEM((NZ, 16, 128), BF16),
            pltpu.VMEM((NZ - 1, 16, 128), BF16),
            pltpu.VMEM((2, NS * 2, 128), F32),
            dma((2, PAIRS)),
            dma((PAIRS, NZ + NY - 1)),
            dma((PAIRS, NZ + NY - 1)),
            dma((NZ + NY - 1,)),
            dma((NZ + NY - 1,)),
            dma((PAIRS, NX - 1)),
            dma((PAIRS, NX - 1)),
            dma((PAIRS, NH - 1)),
            dma((PAIRS, NH - 1)),
            dma((PAIRS,)),
            dma((PAIRS,)),
            dma((PAIRS, NY - 1)),
            dma((PAIRS, NY - 1)),
            dma((PAIRS, NZ - 1)),
            dma((PAIRS, NZ - 1)),
            dma((NZ - 1,)),
            dma((NZ - 1,)),
        ]
        return pl.pallas_call(
            functools.partial(kernel, sizes),
            out_shape=(
                jax.ShapeDtypeStruct((HB, 512), BF16),
                jax.ShapeDtypeStruct((1, 18, 512), BF16),
                jax.ShapeDtypeStruct((1, 18, 512), BF16),
            ),
            in_specs=[sm, vm, vm, anywhere, anywhere],
            out_specs=(vm, vm, vm),
            scratch_shapes=scratch,
            compiler_params=pltpu.CompilerParams(
                collective_id=0, has_side_effects=True, vmem_limit_bytes=58 * 1024 * 1024
            ),
        )(block_mask, keys, values, queries, grad_out)

    return body


def build(mesh, sizes):
    return jax.shard_map(
        body_of(sizes),
        mesh=mesh,
        in_specs=(
            P("lab", None),
            P("img", "lab", None),
            P("img", "lab", None),
            P("img", "lab", None),
            P("lab", "img"),
        ),
        out_specs=(P(("lab", "img"), None), P("img", "lab", None), P("img", "lab", None)),
        check_vma=False,
    )


def solution(mesh):
    return build(mesh, SIZES)
```

time: 576 us -> 76.6 us (0.13)
  blocking collectives: 341 us -> 0 us
  matrix products: 157 us -> 0 us
  Pallas kernels: 0 us -> 70.7 us
  local copies, waits for them, and re-layouts: 35.8 us -> 4.16 us
  waiting for transfers between devices: 24.9 us -> 0 us
  between operations: 14.8 us -> 0.65 us
    unnamed x1 -> x0, blocking collectives: 252 us -> none
    dot_general x32 -> x0, matrix products: 129 us -> none  [the longest x8 43.4 us: run_block(): jnp.einsum('lhp,lhe->phe', dscores, query_block, preferred_element_type=j...]
    all_gather x2 -> x0, blocking collectives: 88.9 us -> none  [the longest x1 47.8 us: body(): lax.all_gather(keys, 'lab', axis=1, tiled=True)]
    pallas_call x0 -> x1, Pallas kernels: none -> 70.7 us  [body(): pl.pallas_call(functools.partial(kernel, sizes), out_shape=(jax.ShapeDtyp...]
    sub x8 -> x0, matrix products: 28.7 us -> none  [attend(): probs = jax.nn.softmax(scores, axis=-1)]
    unnamed x2 -> x0, waiting for transfers between devices: 24.9 us -> none
    unnamed x21 -> x8, local copies, waits for them, and re-layouts: 18.1 us -> 4.16 us
  transfers between devices with their start and end apart: 1 -> 0, of which waited for: 1 -> 0; matrix products, arithmetic and copies ran while one was open for 1% -> 0% of each run, Pallas kernels for 0% -> 0%
where the time goes in v1:
time: 76.6 us; the launch traced here: 75.5 us
  Pallas kernels  70.7 us (92%)
  local copies, waits for them, and re-layouts  4.16 us (5%)
    pallas_call x1, Pallas kernels, body(): pl.pallas_call(functools.partial(kernel, sizes), out_shape=(jax.ShapeDtyp...  70.7 us
    unnamed x8, local copies, waits for them, and re-layouts  4.16 us

profile of v1, /device:TPU:6, one launch (start us, length us, event | category | flops | bytes accessed | tf_op | source)
XLA Modules:
  0.0 75.5 jit_solution(13989074053756857016)
XLA Ops:
  0.6 1.3 %copy.8.mask_ref = s32[8,1]{1,0:T(8,128)} copy(s32[8,1]{0,1:T(1,128)} %param.9) | data formatting | bytes 64 | tf_op args[4]
  2.0 70.7 %shard_map.76 = (bf16[64,512]{1,0:T(8,128)(2,1)}, bf16[1,18,512]{2,1,0:T(8,128)(2,1)}, bf16[1,18,512]{2,1,0:T(8,128)(2,1)}) custom-call(s32[8,1]{1,0:T(8,128)} %copy.8.mask_ref, bf16[1,18,512]{2,1,0:T(8,128)(2,1)} %key_ref.1, bf16[1,18,512]{2,1,0:T(8,128)(2,1)} %val_ref.1, bf16[1024,512]{1,0:T(8,128)(2,1)} %q_hbm.1, bf16[1,1024,512]{2,1,0:T(8,128)(2,1)} %g_hbm.1), custom_call_target="tpu_custom_call" | custom-call | tf_op jit(solution)/shard_map/pallas_call | solution.py:560
  72.7 0.0 copy-start.1
  72.7 1.5 %copy.12 = bf16[64,512]{1,0:T(8,128)(2,1)} copy(bf16[64,512]{1,0:T(8,128)(2,1)} %get-tuple-element.6) | data formatting | bytes 131072
  74.2 0.0 copy-done.1
  74.2 0.0 copy-start
  74.2 0.6 copy.13
  74.8 0.1 copy-done
  74.9 0.6 copy.14
Async XLA Ops:
  72.7 1.5 %copy-start.1 = (bf16[1,18,512]{2,1,0:T(8,128)(2,1)S(1)}, bf16[1,18,512]{2,1,0:T(8,128)(2,1)}, u32[]{:S(2)}) copy-start(bf16[1,18,512]{2,1,0:T(8,128)(2,1)} %get-tuple-element.7) | copy-start | bytes 55300
  74.2 0.7 copy-start

commit v2 on v1

--- a/solution.py
+++ b/solution.py
@@ -52,17 +52,20 @@
     ra,
     sb,
     rb,
-    tb,
     sc,
     rc,
-    st,
-    rt,
-    ft,
+    g0,
+    sd,
+    rd,
+    in_order,
+    out_order,
     in_sem,
     ag_send,
     ag_recv,
-    agt_send,
-    agt_recv,
+    g_send,
+    g_recv,
+    gc_send,
+    gc_recv,
     x_send,
     x_recv,
     h_send,
@@ -73,8 +76,8 @@
     b_recv,
     c_send,
     c_recv,
-    t_send,
-    t_recv,
+    d_send,
+    d_recv,
 ):
     NZ, NY, NX, NH = sizes
     NS = NZ * NY
@@ -86,7 +89,8 @@
     ZR = NZ * 16
     HALF = NS * 16
     TH = NS * 2
-    TZ = NZ * 2
+    BLOCK = 48
+    last = PAIRS - 1
 
     a = lax.axis_index("lab")
     i = lax.axis_index("img")
@@ -109,6 +113,9 @@
     def dev_y(d):
         return lab_id(z, (y + d) % NY, c)
 
+    def dev_s(d):
+        return lab_id((z + d % NZ) % NZ, (y + d // NZ) % NY, c)
+
     def dev_c():
         return lab_id(z, y, 1 - c)
 
@@ -124,8 +131,7 @@
         )
 
     peers = [dev_c()]
-    peers += [dev_z(d) for d in range(1, NZ)]
-    peers += [dev_y(d) for d in range(1, NY)]
+    peers += [dev_s(d) for d in range(1, NS)]
     peers += [dev_x(d) for d in range(1, NX)]
     peers += [dev_h(d) for d in range(1, NH)]
     barrier = pltpu.get_barrier_semaphore()
@@ -143,12 +149,29 @@
         for cp in in_copies(j):
             cp.start()
 
+    mine = pl.multiple_of(slot * BLOCK, 16)
     for n, ref in ((0, key_ref), (1, val_ref)):
         for j in range(PAIRS):
             lanes = slice(j * 128, (j + 1) * 128)
-            kv[j, n, pl.ds(pl.multiple_of(slot * 16, 16), 16), :] = ref[0, 0:16, lanes]
+            if j == 0:
+                g0[pl.ds(mine + n * 16, 16), :] = ref[0, 0:16, lanes]
+            else:
+                kv[j, n, pl.ds(pl.multiple_of(slot * 16, 16), 16), :] = ref[0, 0:16, lanes]
             tl_f[pl.ds(n * 8 + j * 2, 2), :] = ref[0, 16:18, lanes].astype(F32)
-    tl[pl.ds(pl.multiple_of(slot * 16, 16), 16), :] = tl_f[...].astype(BF16)
+    g0[pl.ds(mine + 32, 16), :] = tl_f[...].astype(BF16)
+
+    per = 2 * NLAB
+    row = lax.broadcasted_iota(jnp.int32, (16 * NLAB, 16 * NLAB), 0)
+    col = lax.broadcasted_iota(jnp.int32, (16 * NLAB, 16 * NLAB), 1)
+    want = ((row % per) // 2) * 16 + ((row // per) % 2) * 8 + (row // (2 * per)) * 2 + row % 2
+    in_order[...] = jnp.where(col == want, 1.0, 0.0).astype(BF16)
+    row = lax.broadcasted_iota(jnp.int32, (16 * NS, 16 * NS), 0)
+    col = lax.broadcasted_iota(jnp.int32, (16 * NS, 16 * NS), 1)
+    want = ((row // 4) % PAIRS) * (2 * TH) + ((row // 2) % 2) * TH + (row // 16) * 2 + row % 2
+    out_order[...] = jnp.where(col == want, 1.0, 0.0).astype(BF16)
+    for j in range(PAIRS):
+        for n in range(2):
+            acc[j, n] = jnp.zeros((ROWS, 128), F32)
     pl.semaphore_wait(barrier, len(peers))
 
     def ag_z(j, d):
@@ -165,19 +188,14 @@
         n = NZ + NY - 2
         return rcopy(r, r, ag_send.at[j, n], ag_recv.at[j, n], dev_c())
 
-    def agt_z(d):
-        r = tl.at[pl.ds(pl.multiple_of(slot * 16, 16), 16), :]
-        return rcopy(r, r, agt_send.at[d - 1], agt_recv.at[d - 1], dev_z(d))
-
-    def agt_y(d):
-        r = tl.at[pl.ds(pl.multiple_of(c * HALF + y * ZR, 16), ZR), :]
-        n = NZ - 1 + d - 1
-        return rcopy(r, r, agt_send.at[n], agt_recv.at[n], dev_y(d))
-
-    def agt_c():
-        r = tl.at[pl.ds(pl.multiple_of(c * HALF, 16), HALF), :]
-        n = NZ + NY - 2
-        return rcopy(r, r, agt_send.at[n], agt_recv.at[n], dev_c())
+    def first_s(d):
+        r = g0.at[pl.ds(mine, BLOCK), :]
+        return rcopy(r, r, g_send.at[d - 1], g_recv.at[d - 1], dev_s(d))
+
+    def first_c(d):
+        yy = (y + NY - d) % NY
+        r = g0.at[pl.ds(pl.multiple_of((c * NS + yy * NZ) * BLOCK, 16), NZ * BLOCK), :]
+        return rcopy(r, r, gc_send.at[d], gc_recv.at[d], dev_c())
 
     def z_to_y(j):
         for d in range(1, NZ):
@@ -190,37 +208,25 @@
             ag_y(j, d).wait_recv()
         ag_c(j).start()
 
-    for d in range(1, NZ):
-        agt_z(d).start()
-        ag_z(0, d).start()
+    for d in range(1, NS):
+        first_s(d).start()
     for j in range(1, PAIRS):
         for d in range(1, NZ):
             ag_z(j, d).start()
-
-    for j in range(PAIRS):
-        for n in range(2):
-            acc[j, n] = jnp.zeros((ROWS, 128), F32)
-
-    for d in range(1, NZ):
-        agt_z(d).wait_recv()
-    for d in range(1, NY):
-        agt_y(d).start()
-    z_to_y(0)
-    z_to_y(1)
-    tails = 16 * NLAB
-    row = lax.broadcasted_iota(jnp.int32, (tails, tails), 0)
-    col = lax.broadcasted_iota(jnp.int32, (tails, tails), 1)
-    per = 2 * NLAB
-    want = ((row % per) // 2) * 16 + ((row // per) % 2) * 8 + (row // (2 * per)) * 2 + row % 2
-    order = jnp.where(col == want, 1.0, 0.0).astype(BF16)
-    for d in range(1, NY):
-        agt_y(d).wait_recv()
-    agt_c().start()
-    y_to_c(0)
-    for j in range(2, PAIRS):
+    for g in range(NY):
+        for d in range(g * NZ, (g + 1) * NZ):
+            if d > 0:
+                first_s(d).wait_recv()
+        first_c(g).start()
+    for j in range(1, PAIRS):
         z_to_y(j)
-    agt_c().wait_recv()
-    placed = dot(order, tl[...], 1, 0).astype(BF16)
+    for g in range(NY):
+        first_c(g).wait_recv()
+    for n in range(NLAB):
+        for u in range(2):
+            kv[0, u, n * 16 : (n + 1) * 16, :] = g0[n * BLOCK + u * 16 : n * BLOCK + (u + 1) * 16, :]
+        tl[n * 16 : (n + 1) * 16, :] = g0[n * BLOCK + 32 : (n + 1) * BLOCK, :]
+    placed = dot(in_order[...], tl[...], 1, 0).astype(BF16)
     for j in range(PAIRS):
         for n in range(2):
             b0 = (j * 2 + n) * per
@@ -230,7 +236,6 @@
         kt[j] = jnp.transpose(kv[j, 0].astype(F32)).astype(BF16)
 
     def ready(j):
-        ag_c(j).wait_recv()
         for cp in in_copies(j):
             cp.wait()
         turn_keys(j)
@@ -280,8 +285,9 @@
     def rs_c(j, d):
         return rcopy(sc.at[j, d - 1], rc.at[j, d - 1], c_send.at[j, d - 1], c_recv.at[j, d - 1], dev_z(d))
 
-    def rs_t(d):
-        return rcopy(st.at[(z + d) % NZ], rt.at[d - 1], t_send.at[d - 1], t_recv.at[d - 1], dev_z(d))
+    def rs_d(d):
+        to = (y + d // NZ) % NY * NZ + (z + d % NZ) % NZ
+        return rcopy(sd.at[to], rd.at[d - 1], d_send.at[d - 1], d_recv.at[d - 1], dev_s(d))
 
     def stage_a(j):
         other = 1 - c
@@ -296,28 +302,15 @@
         rs_a(j).wait_recv()
         for d in list(range(1, NY)) + [0]:
             yy = (y + d) % NY
-            tail = []
             for n in range(2):
                 at = pl.ds(pl.multiple_of(c * HALF + yy * ZR, 16), ZR)
                 got = ra[j, n, pl.ds(pl.multiple_of(yy * ZR, 16), ZR), :].astype(F32)
                 both = acc[j, n, at, :] + got
-                tat = pl.ds(pl.multiple_of(MAIN + c * TH + yy * TZ, 8), TZ)
-                tail.append(acc[j, n, tat, :])
                 if d == 0:
                     acc[j, n, at, :] = both
                 else:
                     sb[j, d - 1, n * ZR : (n + 1) * ZR, :] = both.astype(BF16)
-            tmine = jnp.concatenate(tail, axis=0)
-            for n in range(2):
-                full = ra[j, n, HALF : HALF + TH, :].astype(F32)
-                ft[n] = full
-            tgot = jnp.concatenate(
-                [ft[n, pl.ds(pl.multiple_of(yy * TZ, 8), TZ), :] for n in range(2)], axis=0
-            )
-            if d == 0:
-                tb[j] = tmine + tgot
-            else:
-                sb[j, d - 1, 2 * ZR : 2 * ZR + 2 * TZ, :] = (tmine + tgot).astype(BF16)
+            if d > 0:
                 rs_b(j, d).start()
 
     def stage_c(j):
@@ -329,16 +322,53 @@
             for d in range(1, NY):
                 v = v + rb[j, d - 1, n * ZR : (n + 1) * ZR, :].astype(F32)
             acc[j, n, at, :] = v
-        v = tb[j]
-        for d in range(1, NY):
-            v = v + rb[j, d - 1, 2 * ZR : 2 * ZR + 2 * TZ, :].astype(F32)
-        tb[j] = v
         for d in range(1, NZ):
             zz = (z + d) % NZ
             for n in range(2):
                 at = pl.ds(pl.multiple_of(c * HALF + y * ZR + zz * 16, 16), 16)
                 sc[j, d - 1, n * 16 : (n + 1) * 16, :] = acc[j, n, at, :].astype(BF16)
             rs_c(j, d).start()
+
+    def stage_d():
+        rs_a(last).wait_recv()
+        tails = []
+        for j in range(PAIRS):
+            for n in range(2):
+                t = acc[j, n, pl.ds(pl.multiple_of(MAIN + c * TH, 16), TH), :]
+                tails.append((t + ra[j, n, HALF : HALF + TH, :].astype(F32)).astype(BF16))
+        moved = dot(out_order[...], jnp.concatenate(tails, axis=0), 1, 0).astype(BF16)
+        for n in range(2):
+            at = pl.ds(pl.multiple_of(c * HALF, 16), HALF)
+            v = acc[last, n, at, :] + ra[last, n, 0:HALF, :].astype(F32)
+            acc[last, n, at, :] = v
+            v = v.astype(BF16)
+            for u in range(NS):
+                sd[u, n * 16 : (n + 1) * 16, :] = v[u * 16 : (u + 1) * 16, :]
+        for u in range(NS):
+            sd[u, 32:48, :] = moved[u * 16 : (u + 1) * 16, :]
+        for d in range(1, NS):
+            rs_d(d).start()
+
+    def final_d():
+        for d in range(1, NS):
+            rs_d(d).wait_recv()
+        for n, out in ((0, dk_out), (1, dv_out)):
+            v = acc[last, n, pl.ds(pl.multiple_of(slot * 16, 16), 16), :]
+            for d in range(1, NS):
+                v = v + rd[d - 1, n * 16 : (n + 1) * 16, :].astype(F32)
+            if n == 0:
+                v = v * SCALE
+            out[0, 0:16, last * 128 : PAIRS * 128] = v.astype(BF16)
+        v = sd[y * NZ + z, 32:48, :].astype(F32)
+        for d in range(1, NS):
+            v = v + rd[d - 1, 32:48, :].astype(F32)
+        tl_f[...] = v
+        for n, out in ((0, dk_out), (1, dv_out)):
+            for j in range(PAIRS):
+                piece = tl_f[pl.ds(j * 4 + n * 2, 2), :]
+                if n == 0:
+                    piece = piece * SCALE
+                out[0, 16:18, j * 128 : (j + 1) * 128] = piece.astype(BF16)
 
     def final_kv(j):
         for d in range(1, NZ):
@@ -391,12 +421,13 @@
 
         @pl.when(jnp.logical_and(t == NX - 1, j < PAIRS - 1))
         def _():
+            ag_c(j + 1).wait_recv()
             ready(j + 1)
 
         _, chunk, q, g = operands(s)
         m = jnp.concatenate(
             [
-                jnp.full((1, 128), mask_ref[chunk * (CH // 128) + b, 0], jnp.int32).astype(F32)
+                jnp.full((1, 128), mask_ref[0, chunk * (CH // 128) + b], jnp.int32).astype(F32)
                 for b in range(CH // 128)
             ],
             axis=1,
@@ -424,74 +455,64 @@
             dq_own[j, 64:128, :] = dq1
             stage_a(j)
 
-        @pl.when(jnp.logical_and(t == 0, j > 0))
+        @pl.when(jnp.logical_and(t == min(1, NX - 1), j > 0))
         def _():
             stage_h(j - 1)
             stage_b(j - 1)
 
-        @pl.when(jnp.logical_and(t == max(NX - 2, 1), j > 0))
-        def _():
-            stage_c(j - 1)
-
-        @pl.when(jnp.logical_and(t == NX - 1, j > 0))
-        def _():
-            final_kv(j - 1)
-            final_q(j - 1)
+        @pl.when(jnp.logical_and(t == min(2, NX - 1), j > 1))
+        def _():
+            stage_c(j - 2)
+
+        @pl.when(jnp.logical_and(t == NX - 1, j > 1))
+        def _():
+            final_q(j - 2)
+
+        @pl.when(jnp.logical_and(t == NX - 1, j > 2))
+        def _():
+            final_kv(j - 3)
 
         return carry
 
     lax.fori_loop(0, STEPS, body, 0)
 
-    last = PAIRS - 1
     stage_h(last)
-    stage_b(last)
-    stage_c(last)
-    n_t = PAIRS * 2 * TZ
-    row = lax.broadcasted_iota(jnp.int32, (n_t, n_t), 0)
-    col = lax.broadcasted_iota(jnp.int32, (n_t, n_t), 1)
-    want = ((row // 4) % PAIRS) * (2 * TZ) + ((row // 2) % 2) * TZ + (row // 16) * 2 + row % 2
-    order = jnp.where(col == want, 1.0, 0.0).astype(BF16)
-    mine = jnp.concatenate([tb[j].astype(BF16) for j in range(PAIRS)], axis=0)
-    sorted_tails = dot(order, mine, 1, 0).astype(BF16)
-    for zz in range(NZ):
-        st[zz] = sorted_tails[zz * 16 : (zz + 1) * 16, :]
-    for d in range(1, NZ):
-        rs_t(d).start()
-    final_kv(last)
-    for d in range(1, NZ):
-        rs_t(d).wait_recv()
-    v = st[z].astype(F32)
-    for d in range(1, NZ):
-        v = v + rt[d - 1].astype(F32)
-    tl_f[...] = v
-    for n, out in ((0, dk_out), (1, dv_out)):
-        for j in range(PAIRS):
-            piece = tl_f[pl.ds(j * 4 + n * 2, 2), :]
-            if n == 0:
-                piece = piece * SCALE
-            out[0, 16:18, j * 128 : (j + 1) * 128] = piece.astype(BF16)
+    stage_d()
+    stage_c(PAIRS - 2)
+    final_kv(PAIRS - 3)
+    final_q(PAIRS - 2)
+    final_kv(PAIRS - 2)
+    final_d()
     final_q(last)
 
-    for d in range(1, NZ):
-        agt_z(d).wait_send()
-        rs_t(d).wait_send()
-    for d in range(1, NY):
-        agt_y(d).wait_send()
-    agt_c().wait_send()
+    for d in range(1, NS):
+        first_s(d).wait_send()
+        rs_d(d).wait_send()
+    for g in range(NY):
+        first_c(g).wait_send()
 
     def drain(j, carry):
-        for d in range(1, NZ):
-            ag_z(j, d).wait_send()
-            rs_c(j, d).wait_send()
-        for d in range(1, NY):
-            ag_y(j, d).wait_send()
-            rs_b(j, d).wait_send()
-        ag_c(j).wait_send()
         rs_a(j).wait_send()
         for t in range(NX - 1):
             rs_x(j, t).wait_send()
         for d in range(1, NH):
             rs_h(j, d).wait_send()
+
+        @pl.when(j > 0)
+        def _():
+            for d in range(1, NZ):
+                ag_z(j, d).wait_send()
+            for d in range(1, NY):
+                ag_y(j, d).wait_send()
+            ag_c(j).wait_send()
+
+        @pl.when(j < last)
+        def _():
+            for d in range(1, NY):
+                rs_b(j, d).wait_send()
+            for d in range(1, NZ):
+                rs_c(j, d).wait_send()
+
         return carry
 
     lax.fori_loop(0, PAIRS, drain, 0)
@@ -504,7 +525,7 @@
     ROWS = 18 * NLAB
     HB = CH // NH
     LABELS = CH * NX
-    ZR, TZ = NZ * 16, NZ * 2
+    ZR = NZ * 16
     dma = pltpu.SemaphoreType.DMA
 
     def body(queries, keys, values, grad_out, block_mask):
@@ -531,19 +552,22 @@
             pltpu.VMEM((PAIRS, CH, 128), F32),
             pltpu.VMEM((PAIRS, 2, NS * 18, 128), BF16),
             pltpu.VMEM((PAIRS, 2, NS * 18, 128), BF16),
-            pltpu.VMEM((PAIRS, NY - 1, 2 * ZR + 2 * TZ, 128), BF16),
-            pltpu.VMEM((PAIRS, NY - 1, 2 * ZR + 2 * TZ, 128), BF16),
-            pltpu.VMEM((PAIRS, 2 * TZ, 128), F32),
+            pltpu.VMEM((PAIRS, NY - 1, 2 * ZR, 128), BF16),
+            pltpu.VMEM((PAIRS, NY - 1, 2 * ZR, 128), BF16),
             pltpu.VMEM((PAIRS, NZ - 1, 32, 128), BF16),
             pltpu.VMEM((PAIRS, NZ - 1, 32, 128), BF16),
-            pltpu.VMEM((NZ, 16, 128), BF16),
-            pltpu.VMEM((NZ - 1, 16, 128), BF16),
-            pltpu.VMEM((2, NS * 2, 128), F32),
+            pltpu.VMEM((NLAB * 48, 128), BF16),
+            pltpu.VMEM((NS, 48, 128), BF16),
+            pltpu.VMEM((NS - 1, 48, 128), BF16),
+            pltpu.VMEM((16 * NLAB, 16 * NLAB), BF16),
+            pltpu.VMEM((16 * NS, 16 * NS), BF16),
             dma((2, PAIRS)),
             dma((PAIRS, NZ + NY - 1)),
             dma((PAIRS, NZ + NY - 1)),
-            dma((NZ + NY - 1,)),
-            dma((NZ + NY - 1,)),
+            dma((NS - 1,)),
+            dma((NS - 1,)),
+            dma((NY,)),
+            dma((NY,)),
             dma((PAIRS, NX - 1)),
             dma((PAIRS, NX - 1)),
             dma((PAIRS, NH - 1)),
@@ -554,10 +578,10 @@
             dma((PAIRS, NY - 1)),
             dma((PAIRS, NZ - 1)),
             dma((PAIRS, NZ - 1)),
-            dma((NZ - 1,)),
-            dma((NZ - 1,)),
+            dma((NS - 1,)),
+            dma((NS - 1,)),
         ]
-        return pl.pallas_call(
+        outs = pl.pallas_call(
             functools.partial(kernel, sizes),
             out_shape=(
                 jax.ShapeDtypeStruct((HB, 512), BF16),
@@ -570,7 +594,8 @@
             compiler_params=pltpu.CompilerParams(
                 collective_id=0, has_side_effects=True, vmem_limit_bytes=58 * 1024 * 1024
             ),
-        )(block_mask, keys, values, queries, grad_out)
+        )(block_mask.T, keys, values, queries, grad_out)
+        return outs
 
     return body
 

time: 76.6 us -> 66.6 us (0.87)
  Pallas kernels: 70.7 us -> 62.4 us
  local copies, waits for them, and re-layouts: 4.16 us -> 2.84 us
    pallas_call x1, Pallas kernels: 70.7 us -> 62.4 us  [body(): pl.pallas_call(functools.partial(kernel, sizes), out_shape=(jax.ShapeDtyp...]
    unnamed x8 -> x7, local copies, waits for them, and re-layouts: 4.16 us -> 2.84 us
where the time goes in v2:
time: 66.6 us; the launch traced here: 65.9 us
  Pallas kernels  62.4 us (94%)
  local copies, waits for them, and re-layouts  2.84 us (4%)
    pallas_call x1, Pallas kernels, body(): pl.pallas_call(functools.partial(kernel, sizes), out_shape=(jax.ShapeDtyp...  62.4 us
    unnamed x7, local copies, waits for them, and re-layouts  2.84 us

profile of v2, /device:TPU:6, one launch (start us, length us, event | category | flops | bytes accessed | tf_op | source)
XLA Modules:
  0.0 65.9 jit_solution(17480430610902637110)
XLA Ops:
  0.6 62.4 %shard_map.76 = (bf16[64,512]{1,0:T(8,128)(2,1)}, bf16[1,18,512]{2,1,0:T(8,128)(2,1)}, bf16[1,18,512]{2,1,0:T(8,128)(2,1)}) custom-call(s32[1,8]{1,0:T(1,128)} %bitcast.1, bf16[1,18,512]{2,1,0:T(8,128)(2,1)} %key_ref.1, bf16[1,18,512]{2,1,0:T(8,128)(2,1)} %val_ref.1, bf16[1024,512]{1,0:T(8,128)(2,1)} %q_hbm.1, bf16[1,1024,512]{2,1,0:T(8,128)(2,1)} %g_hbm.1), custom_call_target="tpu_custom_call" | custom-call | tf_op jit(solution)/shard_map/pallas_call | solution.py:584
  63.0 0.0 copy-start.1
  63.0 1.5 %copy.11 = bf16[64,512]{1,0:T(8,128)(2,1)} copy(bf16[64,512]{1,0:T(8,128)(2,1)} %get-tuple-element.6) | data formatting | bytes 131072
  64.5 0.0 copy-done.1
  64.5 0.0 copy-start
  64.5 0.6 copy.12
  65.1 0.1 copy-done
  65.3 0.6 copy.13
Async XLA Ops:
  63.0 1.5 %copy-start.1 = (bf16[1,18,512]{2,1,0:T(8,128)(2,1)S(1)}, bf16[1,18,512]{2,1,0:T(8,128)(2,1)}, u32[]{:S(2)}) copy-start(bf16[1,18,512]{2,1,0:T(8,128)(2,1)} %get-tuple-element.7) | copy-start | bytes 55300
  64.5 0.7 %copy-start = (bf16[1,18,512]{2,1,0:T(8,128)(2,1)S(1)}, bf16[1,18,512]{2,1,0:T(8,128)(2,1)}, u32[]{:S(2)}) copy-start(bf16[1,18,512]{2,1,0:T(8,128)(2,1)} %get-tuple-element.8) | copy-start | bytes 55300

commit v3 on v2

--- a/solution.py
+++ b/solution.py
@@ -24,13 +24,15 @@
 def kernel(
     sizes,
     mask_ref,
-    key_ref,
-    val_ref,
+    key_hbm,
+    val_hbm,
     q_hbm,
     g_hbm,
     dq_out,
     dk_out,
     dv_out,
+    key_ref,
+    val_ref,
     q_v,
     g_v,
     kv,
@@ -60,6 +62,7 @@
     in_order,
     out_order,
     in_sem,
+    kv_sem,
     ag_send,
     ag_recv,
     g_send,
@@ -138,6 +141,13 @@
     for dev in peers:
         pl.semaphore_signal(barrier, inc=1, device_id=dev, device_id_type=MESH)
 
+    kv_copies = (
+        pltpu.make_async_copy(key_hbm, key_ref, kv_sem.at[0]),
+        pltpu.make_async_copy(val_hbm, val_ref, kv_sem.at[1]),
+    )
+    for cp in kv_copies:
+        cp.start()
+
     def in_copies(j):
         lanes = pl.ds(pl.multiple_of(j * 128, 128), 128)
         return (
@@ -149,6 +159,31 @@
         for cp in in_copies(j):
             cp.start()
 
+    per = 2 * NLAB
+
+    def log2(n):
+        return n.bit_length() - 1
+
+    row = lax.broadcasted_iota(jnp.int32, (16 * NLAB, 1), 0)
+    want = (
+        (((row & (per - 1)) >> 1) << 4)
+        + (((row >> log2(per)) & 1) << 3)
+        + ((row >> log2(2 * per)) << 1)
+        + (row & 1)
+    )
+    col = lax.broadcasted_iota(jnp.int32, (16 * NLAB, 16 * NLAB), 1)
+    in_order[...] = jnp.where(col == want, 1.0, 0.0).astype(BF16)
+    row = lax.broadcasted_iota(jnp.int32, (16 * NS, 1), 0)
+    want = (
+        (((row >> 2) & (PAIRS - 1)) << log2(2 * TH))
+        + (((row >> 1) & 1) << log2(TH))
+        + ((row >> 4) << 1)
+        + (row & 1)
+    )
+    col = lax.broadcasted_iota(jnp.int32, (16 * NS, 16 * NS), 1)
+    out_order[...] = jnp.where(col == want, 1.0, 0.0).astype(BF16)
+    for cp in kv_copies:
+        cp.wait()
     mine = pl.multiple_of(slot * BLOCK, 16)
     for n, ref in ((0, key_ref), (1, val_ref)):
         for j in range(PAIRS):
@@ -160,18 +195,6 @@
             tl_f[pl.ds(n * 8 + j * 2, 2), :] = ref[0, 16:18, lanes].astype(F32)
     g0[pl.ds(mine + 32, 16), :] = tl_f[...].astype(BF16)
 
-    per = 2 * NLAB
-    row = lax.broadcasted_iota(jnp.int32, (16 * NLAB, 16 * NLAB), 0)
-    col = lax.broadcasted_iota(jnp.int32, (16 * NLAB, 16 * NLAB), 1)
-    want = ((row % per) // 2) * 16 + ((row // per) % 2) * 8 + (row // (2 * per)) * 2 + row % 2
-    in_order[...] = jnp.where(col == want, 1.0, 0.0).astype(BF16)
-    row = lax.broadcasted_iota(jnp.int32, (16 * NS, 16 * NS), 0)
-    col = lax.broadcasted_iota(jnp.int32, (16 * NS, 16 * NS), 1)
-    want = ((row // 4) % PAIRS) * (2 * TH) + ((row // 2) % 2) * TH + (row // 16) * 2 + row % 2
-    out_order[...] = jnp.where(col == want, 1.0, 0.0).astype(BF16)
-    for j in range(PAIRS):
-        for n in range(2):
-            acc[j, n] = jnp.zeros((ROWS, 128), F32)
     pl.semaphore_wait(barrier, len(peers))
 
     def ag_z(j, d):
@@ -210,16 +233,20 @@
 
     for d in range(1, NS):
         first_s(d).start()
-    for j in range(1, PAIRS):
-        for d in range(1, NZ):
-            ag_z(j, d).start()
+    for d in range(1, NZ):
+        ag_z(1, d).start()
     for g in range(NY):
         for d in range(g * NZ, (g + 1) * NZ):
             if d > 0:
                 first_s(d).wait_recv()
         first_c(g).start()
-    for j in range(1, PAIRS):
-        z_to_y(j)
+    z_to_y(1)
+    for j in range(2, PAIRS):
+        for d in range(1, NZ):
+            ag_z(j, d).start()
+    for j in range(PAIRS):
+        for n in range(2):
+            acc[j, n] = jnp.zeros((ROWS, 128), F32)
     for g in range(NY):
         first_c(g).wait_recv()
     for n in range(NLAB):
@@ -268,12 +295,11 @@
         return jnp.sum(e, axis=0, keepdims=True), jnp.sum(e * d_buf[h], axis=0, keepdims=True)
 
     def back(h, j, q, g, m, total, weighted):
-        qm, gm = of_head(h, q), of_head(h, g)
         t = e_buf[h] * (m / total)
         masked = t.astype(BF16)
         ds = (t * (d_buf[h] - weighted / total)).astype(BF16)
-        acc[j, 0] += dot(ds, qm, 1, 0)
-        acc[j, 1] += dot(masked, gm, 1, 0)
+        acc[j, 0] += dot(ds, of_head(h, q), 1, 0)
+        acc[j, 1] += dot(masked, of_head(h, g), 1, 0)
         return dot(kt[j, h * 64 : (h + 1) * 64, :], ds, 1, 0)
 
     def rs_a(j):
@@ -415,11 +441,11 @@
         j = s // NX
         t = s % NX
 
-        @pl.when(jnp.logical_and(t == min(1, NX - 2), j < PAIRS - 1))
+        @pl.when((t == min(2, NX - 2)) & (j < last))
         def _():
             y_to_c(j + 1)
 
-        @pl.when(jnp.logical_and(t == NX - 1, j < PAIRS - 1))
+        @pl.when((t == NX - 1) & (j < last))
         def _():
             ag_c(j + 1).wait_recv()
             ready(j + 1)
@@ -472,6 +498,12 @@
         def _():
             final_kv(j - 3)
 
+        for k in range(2, PAIRS):
+
+            @pl.when(s == min(k - 2, NX - 2))
+            def _():
+                z_to_y(k)
+
         return carry
 
     lax.fori_loop(0, STEPS, body, 0)
@@ -533,6 +565,8 @@
         sm = pl.BlockSpec(memory_space=pltpu.SMEM)
         anywhere = pl.BlockSpec(memory_space=pl.ANY)
         scratch = [
+            pltpu.VMEM((1, 18, 512), BF16),
+            pltpu.VMEM((1, 18, 512), BF16),
             pltpu.VMEM((PAIRS, LABELS, 128), BF16),
             pltpu.VMEM((PAIRS, LABELS, 128), BF16),
             pltpu.VMEM((PAIRS, 2, ROWS, 128), BF16),
@@ -562,6 +596,7 @@
             pltpu.VMEM((16 * NLAB, 16 * NLAB), BF16),
             pltpu.VMEM((16 * NS, 16 * NS), BF16),
             dma((2, PAIRS)),
+            dma((2,)),
             dma((PAIRS, NZ + NY - 1)),
             dma((PAIRS, NZ + NY - 1)),
             dma((NS - 1,)),
@@ -584,11 +619,11 @@
         outs = pl.pallas_call(
             functools.partial(kernel, sizes),
             out_shape=(
-                jax.ShapeDtypeStruct((HB, 512), BF16),
-                jax.ShapeDtypeStruct((1, 18, 512), BF16),
-                jax.ShapeDtypeStruct((1, 18, 512), BF16),
+                pltpu.VMEM((HB, 512), BF16),
+                pltpu.VMEM((1, 18, 512), BF16),
+                pltpu.VMEM((1, 18, 512), BF16),
             ),
-            in_specs=[sm, vm, vm, anywhere, anywhere],
+            in_specs=[sm, anywhere, anywhere, anywhere, anywhere],
             out_specs=(vm, vm, vm),
             scratch_shapes=scratch,
             compiler_params=pltpu.CompilerParams(

time: 66.6 us -> 64.8 us (0.973)
  local copies, waits for them, and re-layouts: 2.84 us -> 1.85 us
    unnamed x7 -> x3, local copies, waits for them, and re-layouts: 2.84 us -> 1.85 us
where the time goes in v3:
time: 64.8 us; the launch traced here: 64.7 us
  Pallas kernels  62.2 us (96%)
  local copies, waits for them, and re-layouts  1.85 us (3%)
    pallas_call x1, Pallas kernels, body(): pl.pallas_call(functools.partial(kernel, sizes), out_shape=(pltpu.VMEM((H...  62.2 us
    unnamed x3, local copies, waits for them, and re-layouts  1.85 us

profile of v3, /device:TPU:6, one launch (start us, length us, event | category | flops | bytes accessed | tf_op | source)
XLA Modules:
  0.0 64.7 jit_solution(15749952395071020807)
XLA Ops:
  0.6 62.2 %shard_map.76 = (bf16[64,512]{1,0:T(8,128)(2,1)S(1)}, bf16[1,18,512]{2,1,0:T(8,128)(2,1)S(1)}, bf16[1,18,512]{2,1,0:T(8,128)(2,1)S(1)}) custom-call(s32[1,8]{1,0:T(1,128)} %bitcast.1, bf16[1,18,512]{2,1,0:T(8,128)(2,1)} %key_hbm.1, bf16[1,18,512]{2,1,0:T(8,128)(2,1)} %val_hbm.1, bf16[1024,512]{1,0:T(8,128)(2,1)} %q_hbm.1, bf16[1,1024,512]{2,1,0:T(8,128)(2,1)} %g_hbm.1), custom_call_target="tpu_custom_call" | custom-call | tf_op jit(solution)/shard_map/pallas_call | solution.py:619
  62.8 0.6 copy.11
  63.4 0.6 copy.12
  64.1 0.6 copy.13

commit v4 on v3

--- a/solution.py
+++ b/solution.py
@@ -81,6 +81,8 @@
     c_recv,
     d_send,
     d_recv,
+    near_sem,
+    far_sem,
 ):
     NZ, NY, NX, NH = sizes
     NS = NZ * NY
@@ -133,13 +135,16 @@
             src_ref=src, dst_ref=dst, send_sem=ssem, recv_sem=rsem, device_id=dev, device_id_type=MESH
         )
 
-    peers = [dev_c()]
-    peers += [dev_s(d) for d in range(1, NS)]
-    peers += [dev_x(d) for d in range(1, NX)]
-    peers += [dev_h(d) for d in range(1, NH)]
     barrier = pltpu.get_barrier_semaphore()
-    for dev in peers:
+    near = [lab_id((z + d % NZ) % NZ, (y + d // NZ) % NY, 0) for d in range(1, NS)]
+    near += [{**lab_id(z, y, 0), **img_id((x + d) % NX, zh)} for d in range(1, NX)]
+    far = [{**lab_id(z, y, 1), **img_id(x, (zh + d) % NH)} for d in range(1, NH)]
+    for dev in near + far:
         pl.semaphore_signal(barrier, inc=1, device_id=dev, device_id_type=MESH)
+
+    @pl.when(c == 1)
+    def _():
+        pl.semaphore_signal(barrier, inc=1, device_id=dev_c(), device_id_type=MESH)
 
     kv_copies = (
         pltpu.make_async_copy(key_hbm, key_ref, kv_sem.at[0]),
@@ -195,7 +200,25 @@
             tl_f[pl.ds(n * 8 + j * 2, 2), :] = ref[0, 16:18, lanes].astype(F32)
     g0[pl.ds(mine + 32, 16), :] = tl_f[...].astype(BF16)
 
-    pl.semaphore_wait(barrier, len(peers))
+
+    @pl.when(c == 0)
+    def _():
+        pl.semaphore_wait(barrier, 2 * len(near) + 1)
+        pl.semaphore_signal(near_sem, inc=1, device_id=dev_c(), device_id_type=MESH)
+
+    @pl.when(c == 1)
+    def _():
+        pl.semaphore_wait(near_sem, 1)
+
+    def far_in():
+        @pl.when(c == 1)
+        def _():
+            pl.semaphore_wait(barrier, 2 * len(far))
+            pl.semaphore_signal(far_sem, inc=1, device_id=dev_c(), device_id_type=MESH)
+
+        @pl.when(c == 0)
+        def _():
+            pl.semaphore_wait(far_sem, 1)
 
     def ag_z(j, d):
         r = kv.at[j, :, pl.ds(pl.multiple_of(slot * 16, 16), 16), :]
@@ -480,6 +503,10 @@
             dq_own[j, 0:64, :] = dq0
             dq_own[j, 64:128, :] = dq1
             stage_a(j)
+
+        @pl.when(s == NX + min(1, NX - 1))
+        def _():
+            far_in()
 
         @pl.when(jnp.logical_and(t == min(1, NX - 1), j > 0))
         def _():
@@ -615,6 +642,8 @@
             dma((PAIRS, NZ - 1)),
             dma((NS - 1,)),
             dma((NS - 1,)),
+            pltpu.SemaphoreType.REGULAR,
+            pltpu.SemaphoreType.REGULAR,
         ]
         outs = pl.pallas_call(
             functools.partial(kernel, sizes),

time: 64.8 us -> 61.3 us (0.946)
  Pallas kernels: 62.2 us -> 58 us
    pallas_call x1, Pallas kernels: 62.2 us -> 58 us  [body(): pl.pallas_call(functools.partial(kernel, sizes), out_shape=(pltpu.VMEM((H...]
where the time goes in v4:
time: 61.3 us; the launch traced here: 60.5 us
  Pallas kernels  58 us (95%)
  local copies, waits for them, and re-layouts  1.85 us (3%)
  between operations  0.64 us (1%)
    pallas_call x1, Pallas kernels, body(): pl.pallas_call(functools.partial(kernel, sizes), out_shape=(pltpu.VMEM((H...  58 us
    unnamed x3, local copies, waits for them, and re-layouts  1.85 us

profile of v4, /device:TPU:6, one launch (start us, length us, event | category | flops | bytes accessed | tf_op | source)
XLA Modules:
  0.0 60.5 jit_solution(1925796405773678523)
XLA Ops:
  0.6 58.0 %shard_map.76 = (bf16[64,512]{1,0:T(8,128)(2,1)S(1)}, bf16[1,18,512]{2,1,0:T(8,128)(2,1)S(1)}, bf16[1,18,512]{2,1,0:T(8,128)(2,1)S(1)}) custom-call(s32[1,8]{1,0:T(1,128)} %bitcast.1, bf16[1,18,512]{2,1,0:T(8,128)(2,1)} %key_hbm.1, bf16[1,18,512]{2,1,0:T(8,128)(2,1)} %val_hbm.1, bf16[1024,512]{1,0:T(8,128)(2,1)} %q_hbm.1, bf16[1,1024,512]{2,1,0:T(8,128)(2,1)} %g_hbm.1), custom_call_target="tpu_custom_call" | custom-call | tf_op jit(solution)/shard_map/pallas_call | solution.py:648
  58.7 0.6 %copy.11 = bf16[64,512]{1,0:T(8,128)(2,1)} copy(bf16[64,512]{1,0:T(8,128)(2,1)S(1)} %get-tuple-element.3) | data formatting | bytes 131072
  59.3 0.6 %copy.12 = bf16[1,18,512]{2,1,0:T(8,128)(2,1)} copy(bf16[1,18,512]{2,1,0:T(8,128)(2,1)S(1)} %get-tuple-element.4) | data formatting | bytes 36864
  59.9 0.6 %copy.13 = bf16[1,18,512]{2,1,0:T(8,128)(2,1)} copy(bf16[1,18,512]{2,1,0:T(8,128)(2,1)S(1)} %get-tuple-element.5) | data formatting | bytes 36864

commit v5 on v4

--- a/solution.py
+++ b/solution.py
@@ -504,14 +504,17 @@
             dq_own[j, 64:128, :] = dq1
             stage_a(j)
 
-        @pl.when(s == NX + min(1, NX - 1))
+        @pl.when(jnp.logical_and(t == min(1, NX - 1), j > 0))
+        def _():
+            stage_b(j - 1)
+
+        @pl.when(s == NX + min(2, NX - 1))
         def _():
             far_in()
 
-        @pl.when(jnp.logical_and(t == min(1, NX - 1), j > 0))
+        @pl.when(jnp.logical_and(t == min(2, NX - 1), j > 0))
         def _():
             stage_h(j - 1)
-            stage_b(j - 1)
 
         @pl.when(jnp.logical_and(t == min(2, NX - 1), j > 1))
         def _():

time: 61.3 us -> 63.3 us (1.033)
  Pallas kernels: 58 us -> 59.6 us
    pallas_call x1, Pallas kernels: 58 us -> 59.6 us  [body(): pl.pallas_call(functools.partial(kernel, sizes), out_shape=(pltpu.VMEM((H...]
where the time goes in v5:
time: 63.3 us; the launch traced here: 62.1 us
  Pallas kernels  59.6 us (94%)
  local copies, waits for them, and re-layouts  1.85 us (3%)
  between operations  0.64 us (1%)
    pallas_call x1, Pallas kernels, body(): pl.pallas_call(functools.partial(kernel, sizes), out_shape=(pltpu.VMEM((H...  59.6 us
    unnamed x3, local copies, waits for them, and re-layouts  1.85 us

profile of v5, /device:TPU:6, one launch (start us, length us, event | category | flops | bytes accessed | tf_op | source)
XLA Modules:
  0.0 62.1 jit_solution(16460800529713371249)
XLA Ops:
  0.6 59.6 %shard_map.76 = (bf16[64,512]{1,0:T(8,128)(2,1)S(1)}, bf16[1,18,512]{2,1,0:T(8,128)(2,1)S(1)}, bf16[1,18,512]{2,1,0:T(8,128)(2,1)S(1)}) custom-call(s32[1,8]{1,0:T(1,128)} %bitcast.1, bf16[1,18,512]{2,1,0:T(8,128)(2,1)} %key_hbm.1, bf16[1,18,512]{2,1,0:T(8,128)(2,1)} %val_hbm.1, bf16[1024,512]{1,0:T(8,128)(2,1)} %q_hbm.1, bf16[1,1024,512]{2,1,0:T(8,128)(2,1)} %g_hbm.1), custom_call_target="tpu_custom_call" | custom-call | tf_op jit(solution)/shard_map/pallas_call | solution.py:651
  60.3 0.6 %copy.11 = bf16[64,512]{1,0:T(8,128)(2,1)} copy(bf16[64,512]{1,0:T(8,128)(2,1)S(1)} %get-tuple-element.3) | data formatting | bytes 131072
  60.9 0.6 copy.12
  61.5 0.6 copy.13
